TPU v7x, 256 devices: a whole 4x4x8 slice. The times are simulated.
256 devices in a mesh: row: 64 (over z, x, core), col: 4 (over y).
Axes of the slice: x: 4, y: 4, z: 8, core: 2. Of those that a mesh axis runs over, the one named last changes fastest.
Arguments:
- eigvecs: float32 [98304, 4096], P('row', 'col'), may hold values from -6 to 6
- reflectors: float32 [2, 98304, 128], P(None, 'row', 'col'), may hold values from -0.0546875 to 0.0546875
- factors: float32 [2, 128, 128], replicated, may hold values from -3 to 3
Outputs:
- transformed: float32 [98304, 4096], P('row', 'col')
All inputs are finite; a program needn't handle non-finite values.
Results may differ from a plain program's by a relative error of at most 0.00012.
Values sent between devices are 32-bit elements; how exact they have to be, the bound alone decides.
A program may use at most 64 MiB of HBM per device.

v0:
```python
import jax
import jax.numpy as jnp
from jax import lax
from jax.sharding import PartitionSpec as P

BLOCKS = 2


def product(left, right):
    return jnp.dot(left, right, precision=lax.Precision.HIGHEST, preferred_element_type=jnp.float32)


def coefficients(partial_value, triangle):
    summed = lax.psum(partial_value, "row")
    return product(triangle, summed)


def body(eigvecs, reflectors, factors):
    triangles = jnp.triu(factors)
    gathered = lax.all_gather(reflectors, "col", axis=2, tiled=True)
    vectors = eigvecs
    for index_block in range(BLOCKS):
        householder = gathered[index_block]
        partial_value = product(householder.T, vectors)
        coefficient = coefficients(partial_value, triangles[index_block])
        vectors = vectors - product(householder, coefficient)
    return vectors


def solution(mesh):
    placed = (P("row", "col"), P(None, "row", "col"), P())
    return jax.shard_map(
        body, mesh=mesh, in_specs=placed, out_specs=P("row", "col"), check_vma=False
    )
```

profile of v0, /device:TPU:1, one launch (start us, length us, event | category | flops | bytes accessed | tf_op | source)
XLA Modules:
  0.0 449.8 jit_solution(7774727432480237867)
XLA Ops:
  6.5 0.0 all-gather.2.cloned.1.call-start
  6.5 0.7 all-gather.2.cloned.1.call-update
  7.3 0.0 all-reduce.3.cloned.1.call-start
  7.3 34.8 %all-gather.2.cloned.1.call-done = f32[2,1536,128]{1,2,0:T(8,128)} async-done(((f32[2,1536,32]{1,2,0:T(8,128)}), f32[2,1536,128]{1,2,0:T(8,128)}) %all-gather.2.cloned.1.call-update) | async-done | bytes 1572880 | tf_op jit(solution)/shard_map/all_gather | solution.py:20
  42.1 7.4 %fusion = f32[128,1024]{1,0:T(8,128)} fusion(f32[1536,1024]{1,0:T(8,128)} %param.3, f32[2,1536,128]{1,2,0:T(8,128)} %all-gather.2.cloned.1.call-done), kind=kOutput, calls=%fused_computation.5 | convolution fusion | flops 2415919104 | bytes 7602176 | tf_op jit(solution)/shard_map/dot_general | solution.py:10
  49.5 0.0 all-reduce.3.cloned.1.call-update
  49.5 0.2 all-reduce.5.cloned.1.call-start
  49.7 0.1 iota_compare_fusion
  49.8 0.0 copy-start.2
  49.8 0.0 copy-start.1
  49.8 6.7 %copy.4 = f32[1536,1024]{0,1:T(8,128)} copy(f32[1536,1024]{1,0:T(8,128)} %param.3) | data formatting | bytes 12582912 | tf_op args[0]
  56.5 0.0 copy-done.2
  56.6 172.5 %all-reduce.3.cloned.1.call-done = f32[128,1024]{1,0:T(8,128)} async-done(((f32[128,1024]{1,0:T(8,128)}), f32[128,1024]{1,0:T(8,128)}) %all-reduce.3.cloned.1.call-update) | async-done | bytes 524304 | tf_op jit(solution)/shard_map/psum | solution.py:14
  229.0 1.6 fusion.2
  230.7 0.0 copy-done.1
  230.7 7.7 %bitcast_subtract_fusion.1 = f32[1536,1024]{0,1:T(8,128)S(1)} fusion(f32[1536,1024]{0,1:T(8,128)} %copy.4, f32[128,1024]{1,0:T(8,128)S(1)} %fusion.2, f32[2,1536,128]{1,2,0:T(8,128)S(1)} %copy-done.1), kind=kOutput, calls=%fused_computation.1 | convolution fusion | flops 2417491968 | bytes 13893632 | tf_op jit(solution)/shard_map/dot_general | solution.py:10
  238.3 0.0 copy-start
  238.4 2.7 copy-done
  241.1 5.8 %convolution_bitcast_fusion = f32[128,1024]{0,1:T(8,128)} fusion(f32[1536,1024]{0,1:T(8,128)S(1)} %bitcast_subtract_fusion.1, f32[2,1536,128]{1,2,0:T(8,128)S(1)} %copy-done.1), kind=kOutput, calls=%fused_computation.2 | convolution fusion | flops 2415919104 | bytes 7602176 | tf_op jit(solution)/shard_map/dot_general | solution.py:10
  246.9 0.0 all-reduce.5.cloned.1.call-update
  246.9 178.8 %all-reduce.5.cloned.1.call-done = f32[128,1024]{0,1:T(8,128)} async-done(((f32[128,1024]{0,1:T(8,128)}), f32[128,1024]{0,1:T(8,128)}) %all-reduce.5.cloned.1.call-update) | async-done | bytes 524304 | tf_op jit(solution)/shard_map/psum | solution.py:14
  425.7 1.6 fusion.1
  427.3 9.4 %bitcast_subtract_fusion = f32[1536,1024]{0,1:T(8,128)} fusion(f32[1536,1024]{0,1:T(8,128)} %copy-done, f32[128,1024]{1,0:T(8,128)S(1)} %fusion.1, f32[2,1536,128]{1,2,0:T(8,128)S(1)} %copy-done.1), kind=kOutput, calls=%fused_computation | convolution fusion | flops 2417491968 | bytes 13893632 | tf_op jit(solution)/shard_map/dot_general | solution.py:10
  436.8 6.6 %copy.5 = f32[1536,1024]{1,0:T(8,128)} copy(f32[1536,1024]{0,1:T(8,128)} %bitcast_subtract_fusion) | data formatting | bytes 12582912 | tf_op jit(solution)/shard_map/sub | solution.py:26
  (2 shorter events, 0.0 us)
Async XLA Ops:
  6.5 35.6 %all-gather.2.cloned.1.call-start = ((), (), s32[]{:S(2)}) async-start(), calls=%async_computation | async-start | bytes 1966080 | tf_op jit(solution)/shard_map/all_gather | solution.py:20
  7.3 221.8 %all-reduce.3.cloned.1.call-start = ((), (), s32[]{:S(2)}) async-start(), calls=%async_computation.1 | async-start | bytes 1048576 | tf_op jit(solution)/shard_map/psum | solution.py:14
  49.5 376.2 %all-reduce.5.cloned.1.call-start = ((), (), s32[]{:S(2)}) async-start(), calls=%async_computation.2 | async-start | bytes 1048576 | tf_op jit(solution)/shard_map/psum | solution.py:14
  49.8 6.7 %copy-start.2 = (f32[2,128,128]{2,1,0:T(8,128)S(1)}, f32[2,128,128]{2,1,0:T(8,128)}, u32[]{:S(2)}) copy-start(f32[2,128,128]{2,1,0:T(8,128)} %param.5) | copy-start | bytes 393220
  49.8 180.8 %copy-start.1 = (f32[2,1536,128]{1,2,0:T(8,128)S(1)}, f32[2,1536,128]{1,2,0:T(8,128)}, u32[]{:S(2)}) copy-start(f32[2,1536,128]{1,2,0:T(8,128)} %all-gather.2.cloned.1.call-done) | copy-start | bytes 4718596
  238.3 2.7 copy-start
Sparse Core Ops, SparseCore 0:
  9.2 32.8 all-gather.1
  49.6 179.3 all-reduce.2
  247.0 178.6 all-reduce.4
where the time goes:
time: 451 us; the launch traced here: 450 us
  waiting for transfers between devices  387 us (86%)
  matrix products  33.5 us (7%)
  local copies, waits for them, and re-layouts  16 us (4%)
  between operations  13.2 us (3%)
    psum x2, waiting for transfers between devices, coefficients(): summed = lax.psum(partial_value, 'row')  351 us
    all_gather x1, waiting for transfers between devices, body(): gathered = lax.all_gather(reflectors, 'col', axis=2, tiled=True)  34.8 us
    dot_general x6, matrix products, product(): jnp.dot(left, right, precision=lax.Precision.HIGHEST, preferred_element_t...  33.5 us
    unnamed x7, local copies, waits for them, and re-layouts  9.4 us
  transfers between devices with their start and end apart: 3, of which 3 were waited for; matrix products, arithmetic and copies ran while one was open for 2% of the time, Pallas kernels for 0%

commit v1 on v0

v1 whole, which is shorter than its diff:
```python
import jax
import jax.numpy as jnp
from jax import lax
from jax.experimental import pallas as pl
from jax.experimental.pallas import tpu as pltpu
from jax.sharding import PartitionSpec as P

MESH = pl.DeviceIdType.MESH
F32, BF16 = jnp.float32, jnp.bfloat16
BLOCKS = 2
X_SIZE, Z_SIZE, Y_SIZE = 4, 8, 4
SETS = 4
CHUNKS = 6

SET_GROUPS = (((0, 0), (0, 1)), ((3, 0), (1, 1)), ((3, 1), (1, 0)), ((2, 0), (2, 1)))


def split(value):
    high = value.astype(BF16)
    return high, (value - high.astype(F32)).astype(BF16)


def dot(left, right, dims):
    return lax.dot_general(left, right, (dims, ((), ())), preferred_element_type=F32)


def product(left, right, dims=((1,), (0,))):
    (lh, ll), (rh, rl) = left, right
    return dot(lh, rh, dims) + (dot(lh, rl, dims) + dot(ll, rh, dims))


def reduce_kernel(
    x_hbm, v_hbm, f_ref, v_out, ch_out, cl_out,
    x_buf, xh, xl, v_all, s_loc, core_in, x_in, x_sum, z_in, s_sum,
    g_loc, g_core, g_xin, g_xsum, g_zin, g_sum,
    x_sem, v_sem, vo_sem, vs_sem, vr_sem,
    c_s, c_r, xs_s, xs_r, zs_s, zs_r, zg_s, zg_r, xg_s, xg_r, cg_s, cg_r,
):
    row, y = lax.axis_index("row"), lax.axis_index("col")
    z, x, core = row // 8, (row // 2) % 4, row % 2
    rows = x_hbm.shape[0] // CHUNKS

    def at(z_, x_, core_, y_):
        return ((z_ * 4 + x_) * 2 + core_, y_)

    other = at(z, x, 1 - core, y)
    x_peer = [at(z, (x + d) % 4, core, y) for d in range(1, 4)]
    z_peer = [at((z + d) % 8, x, core, y) for d in range(1, 8)]
    up, down = at(z, x, core, (y + 1) % 4), at(z, x, core, (y + 3) % 4)
    half = pl.multiple_of(core * 512, 512)
    other_half = pl.multiple_of((1 - core) * 512, 512)

    x_copies = []
    for i in range(CHUNKS):
        part = pl.ds(i * rows, rows)
        copy = pltpu.make_async_copy(x_hbm.at[part], x_buf.at[part], x_sem.at[i])
        copy.start()
        x_copies.append(copy)
    own = pltpu.make_async_copy(v_hbm, v_all.at[0], v_sem)
    own.start()

    barrier = pltpu.get_barrier_semaphore()
    for device in [up, down, other] + x_peer + z_peer:
        pl.semaphore_signal(barrier, inc=1, device_id=device, device_id_type=MESH)
    pl.semaphore_wait(barrier, 13)

    pending = []

    def send(src, dst, s_sem, r_sem, device):
        copy = pltpu.make_async_remote_copy(
            src_ref=src, dst_ref=dst, send_sem=s_sem, recv_sem=r_sem, device_id=device, device_id_type=MESH
        )
        copy.start()
        pending.append(copy)
        return copy

    from_down, from_up, opposite = [None, None], [None, None], [None, None]
    for i in range(2):
        from_down[i] = send(v_hbm.at[i], v_all.at[3, i], vs_sem.at[0, i], vr_sem.at[0, i], up)
        b = 1 - i
        from_up[b] = send(v_hbm.at[b], v_all.at[1, b], vs_sem.at[1, b], vr_sem.at[1, b], down)

    for i in range(CHUNKS):
        x_copies[i].wait()

    @pl.loop(0, CHUNKS)
    def _(i):
        part = pl.ds(pl.multiple_of(i * rows, rows), rows)
        high, low = split(x_buf[part, :])
        xh[part, :] = high
        xl[part, :] = low

    own.wait()

    copies = [{} for _ in range(SETS)]

    def p0(i):
        groups = SET_GROUPS[i]
        vh, vl = split(jnp.concatenate([v_all[r, b] for r, b in groups], axis=0))
        both = jnp.concatenate([vh, vl], axis=0)

        @pl.loop(0, 4)
        def _(j):
            cols = pl.ds(pl.multiple_of(j * 256, 256), 256)
            first = dot(both, xh[:, cols], ((1,), (0,)))
            second = dot(vh, xl[:, cols], ((1,), (0,)))
            s_loc[i, :, cols] = first[:64] + (first[64:] + second)

        copies[i]["c"] = send(
            s_loc.at[i, :, pl.ds(other_half, 512)], core_in.at[i], c_s.at[i], c_r.at[i], other
        )

    def p1(i):
        copies[i]["c"].wait_recv()
        mine = pl.ds(half, 512)
        s_loc[i, :, mine] = s_loc[i, :, mine] + core_in[i]
        copies[i]["x"] = [
            send(
                s_loc.at[i, pl.ds(pl.multiple_of((x + d) % 4 * 16, 16), 16), mine],
                x_in.at[i, d - 1], xs_s.at[i, d - 1], xs_r.at[i, d - 1], x_peer[d - 1],
            )
            for d in range(1, 4)
        ]

    def z_tile(z_):
        return pl.ds(pl.multiple_of(z_ // 4 * 8, 8), 8), pl.ds(pl.multiple_of(z_ % 4 * 128, 128), 128)

    def p2(i):
        for copy in copies[i]["x"]:
            copy.wait_recv()
        mine = s_loc[i, pl.ds(pl.multiple_of(x * 16, 16), 16), pl.ds(half, 512)]
        x_sum[i] = (mine + x_in[i, 0]) + (x_in[i, 1] + x_in[i, 2])
        copies[i]["z"] = []
        for d in range(1, 8):
            tile_rows, tile_cols = z_tile((z + d) % 8)
            copies[i]["z"].append(
                send(
                    x_sum.at[i, tile_rows, tile_cols], z_in.at[i, d - 1],
                    zs_s.at[i, d - 1], zs_r.at[i, d - 1], z_peer[d - 1],
                )
            )

    def groups_of(i):
        return SET_GROUPS[i]

    def group_at(i):
        (r0, b0), (r1, b1) = groups_of(i)
        g = x // 2
        return r0 + g * (r1 - r0), b0 + g * (b1 - b0)

    x_row = x % 2 * 16

    def p3(i):
        for copy in copies[i]["z"]:
            copy.wait_recv()
        tile_rows, tile_cols = z_tile(z)
        total = x_sum[i, tile_rows, tile_cols]
        for d in range(7):
            total = total + z_in[i, d]
        r, b = group_at(i)
        spot = s_sum.at[
            r, b,
            pl.ds(pl.multiple_of(x_row + z // 4 * 8, 8), 8),
            pl.ds(pl.multiple_of(half + z % 4 * 128, 128), 128),
        ]
        spot[...] = total
        copies[i]["zg"] = [
            send(spot, spot, zg_s.at[i, d - 1], zg_r.at[i, d - 1], z_peer[d - 1]) for d in range(1, 8)
        ]

    def p4(i):
        for copy in copies[i]["zg"]:
            copy.wait_recv()
        r, b = group_at(i)
        spot = s_sum.at[r, b, pl.ds(pl.multiple_of(x_row, 16), 16), pl.ds(half, 512)]
        copies[i]["xg"] = [
            send(spot, spot, xg_s.at[i, d - 1], xg_r.at[i, d - 1], x_peer[d - 1]) for d in range(1, 4)
        ]

    def p5(i):
        for copy in copies[i]["xg"]:
            copy.wait_recv()
        copies[i]["cg"] = []
        for k, (r, b) in enumerate(groups_of(i)):
            spot = s_sum.at[r, b, :, pl.ds(half, 512)]
            copies[i]["cg"].append(send(spot, spot, cg_s.at[i, k], cg_r.at[i, k], other))

    def p6(i):
        for copy in copies[i]["cg"]:
            copy.wait_recv()

    def slot(a):
        return (a + Y_SIZE - y) % Y_SIZE

    def g0():
        ordered = [split(jnp.concatenate([v_all[slot(a), b] for a in range(4)], axis=0)) for b in range(2)]
        g_loc[...] = product(ordered[1], ordered[0], ((1,), (1,)))
        spot = g_loc.at[pl.ds(pl.multiple_of((1 - core) * 64, 64), 64)]
        gc["c"] = send(spot, g_core, c_s.at[SETS], c_r.at[SETS], other)

    gc = {}

    def g1():
        gc["c"].wait_recv()
        mine = pl.ds(pl.multiple_of(core * 64, 64), 64)
        g_loc[mine, :] = g_loc[mine, :] + g_core[...]
        gc["x"] = [
            send(
                g_loc.at[pl.ds(pl.multiple_of(core * 64 + (x + d) % 4 * 16, 16), 16)],
                g_xin.at[d - 1], xs_s.at[SETS, d - 1], xs_r.at[SETS, d - 1], x_peer[d - 1],
            )
            for d in range(1, 4)
        ]

    def g2():
        for copy in gc["x"]:
            copy.wait_recv()
        mine = g_loc[pl.ds(pl.multiple_of(core * 64 + x * 16, 16), 16), :]
        g_xsum[...] = (mine + g_xin[0]) + (g_xin[1] + g_xin[2])
        g_zin[z] = g_xsum[...]
        gc["z"] = [
            send(g_xsum, g_zin.at[z], zs_s.at[SETS, d - 1], zs_r.at[SETS, d - 1], z_peer[d - 1])
            for d in range(1, 8)
        ]

    def g3():
        for copy in gc["z"]:
            copy.wait_recv()
        total = g_zin[0]
        for d in range(1, 8):
            total = total + g_zin[d]
        spot = g_sum.at[pl.ds(pl.multiple_of(core * 64 + x * 16, 16), 16)]
        spot[...] = total
        gc["xg"] = [
            send(spot, spot, xg_s.at[SETS, d - 1], xg_r.at[SETS, d - 1], x_peer[d - 1]) for d in range(1, 4)
        ]

    def g4():
        for copy in gc["xg"]:
            copy.wait_recv()
        spot = g_sum.at[pl.ds(pl.multiple_of(core * 64, 64), 64)]
        gc["cg"] = send(spot, spot, cg_s.at[SETS, 0], cg_r.at[SETS, 0], other)

    def g5():
        gc["cg"].wait_recv()

    v_copies = []

    def keep(r, b):
        copy = pltpu.make_async_copy(v_all.at[r, b], v_out.at[r, b], vo_sem.at[r, b])
        copy.start()
        v_copies.append(copy)

    keep(0, 0)
    keep(0, 1)
    p0(0)
    from_down[0].wait_recv()
    opposite[0] = send(v_all.at[3, 0], v_all.at[2, 0], vs_sem.at[2, 0], vr_sem.at[2, 0], up)
    from_up[1].wait_recv()
    opposite[1] = send(v_all.at[1, 1], v_all.at[2, 1], vs_sem.at[2, 1], vr_sem.at[2, 1], down)
    keep(3, 0)
    keep(1, 1)
    p1(0)
    p0(1)
    p2(0)
    p1(1)
    p3(0)
    p2(1)
    p4(0)
    p3(1)
    from_down[1].wait_recv()
    from_up[0].wait_recv()
    keep(3, 1)
    keep(1, 0)
    p0(2)
    p5(0)
    p4(1)
    p1(2)
    p5(1)
    p2(2)
    p3(2)
    opposite[0].wait_recv()
    opposite[1].wait_recv()
    p0(3)
    keep(2, 0)
    keep(2, 1)
    g0()
    p4(2)
    p1(3)
    g1()
    p5(2)
    p2(3)
    g2()
    p3(3)
    g3()
    p4(3)
    g4()
    p5(3)
    g5()
    p6(0)
    p6(1)
    p6(2)
    p6(3)

    upper = lax.broadcasted_iota(jnp.int32, (128, 128), 0) <= lax.broadcasted_iota(jnp.int32, (128, 128), 1)
    t0, t1 = (split(jnp.where(upper, f_ref[b], 0.0)) for b in range(2))
    g = split(g_sum[...])

    for j in range(4):
        cols = pl.ds(j * 256, 256)
        s0, s1 = (jnp.concatenate([s_sum[slot(a), b, :, cols] for a in range(4)], axis=0) for b in range(2))
        c0 = product(t0, split(s0))
        c0 = split(c0)
        c1 = split(product(t1, split(s1 - product(g, c0))))
        for b, (high, low) in enumerate((c0, c1)):
            for a in range(4):
                ch_out[slot(a), b, :, cols] = high[a * 32 : (a + 1) * 32]
                cl_out[slot(a), b, :, cols] = low[a * 32 : (a + 1) * 32]

    for copy in v_copies:
        copy.wait()
    for copy in pending:
        copy.wait_send()


def update_kernel(x_ref, v_ref, ch_ref, cl_ref, out_ref):
    vh, vl = split(v_ref[...])
    dims = ((0,), (0,))
    ch = ch_ref[...]
    out_ref[...] = x_ref[...] - (dot(vh, ch, dims) + (dot(vh, cl_ref[...], dims) + dot(vl, ch, dims)))


def body(eigvecs, reflectors, factors):
    rows, columns = eigvecs.shape
    own = reflectors.transpose(0, 2, 1)
    group = own.shape[1]
    dma = pltpu.SemaphoreType.DMA
    any_space = pl.BlockSpec(memory_space=pl.ANY)
    hbm = pl.BlockSpec(memory_space=pltpu.HBM)
    vmem = pl.BlockSpec(memory_space=pltpu.VMEM)
    v_all, ch, cl = pl.pallas_call(
        reduce_kernel,
        out_shape=[
            jax.ShapeDtypeStruct((Y_SIZE, BLOCKS, group, rows), F32),
            jax.ShapeDtypeStruct((Y_SIZE, BLOCKS, group, columns), BF16),
            jax.ShapeDtypeStruct((Y_SIZE, BLOCKS, group, columns), BF16),
        ],
        in_specs=[hbm, hbm, vmem],
        out_specs=[any_space, vmem, vmem],
        scratch_shapes=[
            pltpu.VMEM((rows, columns), F32),
            pltpu.VMEM((rows, columns), BF16),
            pltpu.VMEM((rows, columns), BF16),
            pltpu.VMEM((Y_SIZE, BLOCKS, group, rows), F32),
            pltpu.VMEM((SETS, 64, columns), F32),
            pltpu.VMEM((SETS, 64, 512), F32),
            pltpu.VMEM((SETS, 3, 16, 512), F32),
            pltpu.VMEM((SETS, 16, 512), F32),
            pltpu.VMEM((SETS, 7, 8, 128), F32),
            pltpu.VMEM((Y_SIZE, BLOCKS, group, columns), F32),
            pltpu.VMEM((128, 128), F32),
            pltpu.VMEM((64, 128), F32),
            pltpu.VMEM((3, 16, 128), F32),
            pltpu.VMEM((16, 128), F32),
            pltpu.VMEM((8, 16, 128), F32),
            pltpu.VMEM((128, 128), F32),
            dma((CHUNKS,)), dma, dma((Y_SIZE, BLOCKS)), dma((3, 2)), dma((3, 2)),
            dma((SETS + 1,)), dma((SETS + 1,)),
            dma((SETS + 1, 3)), dma((SETS + 1, 3)),
            dma((SETS + 1, 7)), dma((SETS + 1, 7)),
            dma((SETS, 7)), dma((SETS, 7)),
            dma((SETS + 1, 3)), dma((SETS + 1, 3)),
            dma((SETS + 1, 2)), dma((SETS + 1, 2)),
        ],
        compiler_params=pltpu.CompilerParams(
            collective_id=0, has_side_effects=True, vmem_limit_bytes=40 * 2**20
        ),
        name="gather_and_reduce",
    )(eigvecs, own, factors)

    depth = Y_SIZE * BLOCKS * group
    step = 256
    return pl.pallas_call(
        update_kernel,
        grid=(rows // step,),
        out_shape=jax.ShapeDtypeStruct((rows, columns), F32),
        in_specs=[
            pl.BlockSpec((step, columns), lambda i: (i, 0)),
            pl.BlockSpec((depth, step), lambda i: (0, i)),
            pl.BlockSpec((depth, columns), lambda i: (0, 0)),
            pl.BlockSpec((depth, columns), lambda i: (0, 0)),
        ],
        out_specs=pl.BlockSpec((step, columns), lambda i: (i, 0)),
        compiler_params=pltpu.CompilerParams(vmem_limit_bytes=32 * 2**20),
        name="update",
    )(eigvecs, v_all.reshape(depth, rows), ch.reshape(depth, columns), cl.reshape(depth, columns))


def solution(mesh):
    placed = (P("row", "col"), P(None, "row", "col"), P())
    return jax.shard_map(
        body, mesh=mesh, in_specs=placed, out_specs=P("row", "col"), check_vma=False
    )
```

time: 451 us -> 86.8 us (0.19)
  waiting for transfers between devices: 387 us -> 0 us
  Pallas kernels: 0 us -> 82 us
  matrix products: 33.5 us -> 0 us
  between operations: 13.2 us -> 0.02 us
  local copies, waits for them, and re-layouts: 16 us -> 4.69 us
    psum x2 -> x0, waiting for transfers between devices: 351 us -> none  [coefficients(): summed = lax.psum(partial_value, 'row')]
    pallas_call x0 -> x2, Pallas kernels: none -> 82 us  [the longest x1 76.5 us: body(): pl.pallas_call(reduce_kernel, out_shape=[jax.ShapeDtypeStruct((Y_SIZE, BL...]
    all_gather x1 -> x0, waiting for transfers between devices: 34.8 us -> none  [body(): gathered = lax.all_gather(reflectors, 'col', axis=2, tiled=True)]
    dot_general x6 -> x0, matrix products: 33.5 us -> none  [product(): jnp.dot(left, right, precision=lax.Precision.HIGHEST, preferred_element_t...]
    sub x1 -> x0, local copies, waits for them, and re-layouts: 6.56 us -> none  [body(): vectors = vectors - product(householder, coefficient)]
    unnamed x7 -> x8, local copies, waits for them, and re-layouts: 9.4 us -> 4.69 us
  transfers between devices with their start and end apart: 3 -> 0, of which waited for: 3 -> 0; matrix products, arithmetic and copies ran while one was open for 2% -> 0% of each run, Pallas kernels for 0% -> 0%
where the time goes in v1:
time: 86.8 us; the launch traced here: 86.7 us
  Pallas kernels  82 us (94%)
  local copies, waits for them, and re-layouts  4.69 us (5%)
    pallas_call x1, Pallas kernels, body(): pl.pallas_call(reduce_kernel, out_shape=[jax.ShapeDtypeStruct((Y_SIZE, BL...  76.5 us
    pallas_call x1, Pallas kernels, body(): pl.pallas_call(update_kernel, grid=(rows // step,), out_shape=jax.ShapeDt...  5.43 us
    unnamed x8, local copies, waits for them, and re-layouts  4.69 us

profile of v1, /device:TPU:1, one launch (start us, length us, event | category | flops | bytes accessed | tf_op | source)
XLA Modules:
  0.0 86.7 jit_solution(4073102609702829755)
XLA Ops:
  0.0 0.0 copy-start
  0.0 2.8 %copy-done = f32[1536,1024]{1,0:T(8,128)S(1)} copy-done((f32[1536,1024]{1,0:T(8,128)S(1)}, f32[1536,1024]{1,0:T(8,128)}, u32[]{:S(2)}) %copy-start) | copy-done | bytes 6291480
  2.8 0.0 copy-start.2
  2.8 1.0 %copy-done.2 = f32[2,1536,32]{1,2,0:T(8,128)S(1)} copy-done((f32[2,1536,32]{1,2,0:T(8,128)S(1)}, f32[2,1536,32]{1,2,0:T(8,128)}, u32[]{:S(2)}) %copy-start.2) | copy-done | bytes 393240
  3.8 0.0 copy-start.3
  3.8 0.9 %copy-done.3 = f32[2,128,128]{2,1,0:T(8,128)S(1)} copy-done((f32[2,128,128]{2,1,0:T(8,128)S(1)}, f32[2,128,128]{2,1,0:T(8,128)}, u32[]{:S(2)}) %copy-start.3) | copy-done | bytes 131096
  4.7 0.0 copy-start.1
  4.7 76.5 %gather_and_reduce.1 = (f32[4,2,32,1536]{3,2,1,0:T(8,128)S(1)}, bf16[4,2,32,1024]{3,2,1,0:T(8,128)(2,1)S(1)}, bf16[4,2,32,1024]{3,2,1,0:T(8,128)(2,1)S(1)}) custom-call(f32[1536,1024]{1,0:T(8,128)S(1)} %copy-done, f32[2,32,1536]{2,1,0:T(8,128)S(1)} %bitcast.7, f32[2,128,128]{2,1,0:T(8,128)S(1)} %copy-done.3), custom_call_target="tpu_custom_call" | custom-call | tf_op jit(solution)/shard_map/gather_and_reduce/pallas_call | solution.py:341
  81.2 0.0 copy-done.1
  81.2 5.4 %update.1 = f32[1536,1024]{1,0:T(8,128)} custom-call(f32[1536,1024]{1,0:T(8,128)S(1)} %copy-done.1, f32[256,1536]{1,0:T(8,128)S(1)} %bitcast.4, bf16[256,1024]{1,0:T(8,128)(2,1)S(1)} %bitcast.5, bf16[256,1024]{1,0:T(8,128)(2,1)S(1)} %bitcast.6), custom_call_target="tpu_custom_call" | custom-call | tf_op jit(solution)/shard_map/update/pallas_call | solution.py:383
Async XLA Ops:
  0.0 2.8 %copy-start = (f32[1536,1024]{1,0:T(8,128)S(1)}, f32[1536,1024]{1,0:T(8,128)}, u32[]{:S(2)}) copy-start(f32[1536,1024]{1,0:T(8,128)} %x_ref.1) | copy-start | bytes 18874372
  2.8 1.0 %copy-start.2 = (f32[2,1536,32]{1,2,0:T(8,128)S(1)}, f32[2,1536,32]{1,2,0:T(8,128)}, u32[]{:S(2)}) copy-start(f32[2,1536,32]{1,2,0:T(8,128)} %param.4) | copy-start | bytes 1179652
  3.8 0.9 %copy-start.3 = (f32[2,128,128]{2,1,0:T(8,128)S(1)}, f32[2,128,128]{2,1,0:T(8,128)}, u32[]{:S(2)}) copy-start(f32[2,128,128]{2,1,0:T(8,128)} %f_ref.1) | copy-start | bytes 393220
  4.7 76.5 %copy-start.1 = (f32[1536,1024]{1,0:T(8,128)S(1)}, f32[1536,1024]{1,0:T(8,128)}, u32[]{:S(2)}) copy-start(f32[1536,1024]{1,0:T(8,128)} %x_ref.1) | copy-start | bytes 18874372

commit v2 on v0

v2 whole, which is shorter than its diff:
```python
import jax
import jax.numpy as jnp
from jax import lax
from jax.experimental import pallas as pl
from jax.experimental.pallas import tpu as pltpu
from jax.sharding import PartitionSpec as P

MESH = pl.DeviceIdType.MESH
F32, BF16 = jnp.float32, jnp.bfloat16
BLOCKS = 2
Y_SIZE = 4
CHUNKS = 6

SET_GROUPS = ((0, 1, 3, 6), (7, 2), (4, 5))
PARTS = ((0, (0, 1)), (0, (3, 6)), (1, (7, 2)), (2, (4, 5)))
SETS = len(SET_GROUPS)


def split(value):
    high = value.astype(BF16)
    return high, (value - high.astype(F32)).astype(BF16)


def dot(left, right, dims):
    return lax.dot_general(left, right, (dims, ((), ())), preferred_element_type=F32)


def product(left, right, dims=((1,), (0,))):
    (lh, ll), (rh, rl) = left, right
    return dot(lh, rh, dims) + (dot(lh, rl, dims) + dot(ll, rh, dims))


def reduce_kernel(
    x_hbm, v_hbm, f_hbm, v_out, ch_out, cl_out,
    x_buf, xh, xl, v_all, f_ref, s_loc, core_in, x_in, x_sum, z_in, z_full, s_sum,
    g_loc, g_core, g_xin, g_zin, g_sum,
    x_sem, v_sem, vo_sem, vs_sem, vr_sem,
    c_s, c_r, xs_s, xs_r, zs_s, zs_r, zg_s, zg_r, xg_s, xg_r, cg_s, cg_r,
):
    row, y = lax.axis_index("row"), lax.axis_index("col")
    z, x, core = row // 8, (row // 2) % 4, row % 2
    rows = x_hbm.shape[0] // CHUNKS

    def at(z_, x_, core_, y_):
        return ((z_ * 4 + x_) * 2 + core_, y_)

    other = at(z, x, 1 - core, y)
    x_peer = [at(z, (x + d) % 4, core, y) for d in range(1, 4)]
    z_peer = [at((z + d) % 8, x, core, y) for d in range(1, 8)]
    up, down = at(z, x, core, (y + 1) % 4), at(z, x, core, (y + 3) % 4)
    mine = pl.ds(pl.multiple_of(core * 512, 512), 512)
    theirs = pl.ds(pl.multiple_of((1 - core) * 512, 512), 512)

    barrier = pltpu.get_barrier_semaphore()
    for device in [up, down, other] + x_peer + z_peer:
        pl.semaphore_signal(barrier, inc=1, device_id=device, device_id_type=MESH)

    x_copies = []
    for i in range(CHUNKS):
        part = pl.ds(i * rows, rows)
        copy = pltpu.make_async_copy(x_hbm.at[part], x_buf.at[part], x_sem.at[i])
        copy.start()
        x_copies.append(copy)
    own = pltpu.make_async_copy(v_hbm, v_all.at[0:2], v_sem.at[0])
    own.start()
    factors = pltpu.make_async_copy(f_hbm, f_ref, v_sem.at[1])
    factors.start()

    def take(i):
        x_copies[i].wait()

        @pl.loop(0, rows // 64)
        def _(j):
            part = pl.ds(pl.multiple_of(i * rows + j * 64, 64), 64)
            high, low = split(x_buf[part, :])
            xh[part, :] = high
            xl[part, :] = low

    for i in range(CHUNKS // 2):
        take(i)

    pl.semaphore_wait(barrier, 13)

    pending = []

    def send(src, dst, s_sem, r_sem, device):
        copy = pltpu.make_async_remote_copy(
            src_ref=src, dst_ref=dst, send_sem=s_sem, recv_sem=r_sem, device_id=device, device_id_type=MESH
        )
        copy.start()
        pending.append(copy)
        return copy

    from_down, from_up, opposite = [None, None], [None, None], [None, None]
    for i in range(2):
        from_down[i] = send(v_hbm.at[i], v_all.at[6 + i], vs_sem.at[0, i], vr_sem.at[0, i], up)
        b = 1 - i
        from_up[b] = send(v_hbm.at[b], v_all.at[2 + b], vs_sem.at[1, b], vr_sem.at[1, b], down)

    for i in range(CHUNKS // 2, CHUNKS):
        take(i)

    own.wait()

    core_copies, x_sends, z_sends, z_shares, x_shares, core_shares = ([[] for _ in range(SETS + 1)] for _ in range(6))
    kept = []

    def arrived(copies):
        for copy in copies:
            copy.wait_recv()

    def partial(k):
        i, groups = PARTS[k]
        base = 32 * SET_GROUPS[i].index(groups[0])
        vh, vl = split(jnp.concatenate([v_all[g] for g in groups], axis=0))
        both = jnp.concatenate([vh, vl], axis=0)

        @pl.loop(0, 4)
        def _(j):
            cols = pl.ds(pl.multiple_of(j * 256, 256), 256)
            first = dot(both, xh[:, cols], ((1,), (0,)))
            second = dot(vh, xl[:, cols], ((1,), (0,)))
            s_loc[i][base : base + 64, cols] = first[:64] + (first[64:] + second)

        here = pl.ds(base, 64)
        core_copies[i].append(send(s_loc[i].at[here, theirs], core_in[i].at[here], c_s.at[k], c_r.at[k], other))
        for g in groups:
            copy = pltpu.make_async_copy(v_all.at[g], v_out.at[g], vo_sem.at[g])
            copy.start()
            kept.append(copy)

    def span(i):
        return 8 * len(SET_GROUPS[i])

    def x_rows(i, x_):
        return pl.ds(pl.multiple_of(x_ * span(i), 16), span(i))

    def to_x(i):
        arrived(core_copies[i])
        s_loc[i][:, mine] = s_loc[i][:, mine] + core_in[i][...]
        for d in range(1, 4):
            x_sends[i].append(
                send(
                    s_loc[i].at[x_rows(i, (x + d) % 4), mine], x_in[i].at[d - 1],
                    xs_s.at[i, d - 1], xs_r.at[i, d - 1], x_peer[d - 1],
                )
            )

    def z_tile(i, z_):
        n = 8 // (span(i) // 8)
        width = 512 // n
        return pl.multiple_of(z_ // n * 8, 8), pl.multiple_of(z_ % n * width, 128), width

    def x_total(i):
        arrived(x_sends[i])
        return (s_loc[i][x_rows(i, x), mine] + x_in[i][0]) + (x_in[i][1] + x_in[i][2])

    def to_z(i):
        x_sum[i][...] = x_total(i)
        for d in range(1, 8):
            r, c, width = z_tile(i, (z + d) % 8)
            z_sends[i].append(
                send(
                    x_sum[i].at[pl.ds(r, 8), pl.ds(c, width)], z_in[i].at[d - 1],
                    zs_s.at[i, d - 1], zs_r.at[i, d - 1], z_peer[d - 1],
                )
            )

    def to_z_whole(i):
        z_full[z] = x_total(i)
        for d in range(1, 8):
            z_sends[i].append(
                send(z_full.at[z], z_full.at[z], zs_s.at[i, d - 1], zs_r.at[i, d - 1], z_peer[d - 1])
            )

    def place(i):
        if i == 0:
            return x * (x + 1) // 2, 0
        g, first = x // 2, pl.multiple_of(x % 2 * 16, 16)
        return (7 - 5 * g if i == 1 else 4 + g), first

    def share_z(i):
        arrived(z_sends[i])
        r, c, width = z_tile(i, z)
        total = x_sum[i][pl.ds(r, 8), pl.ds(c, width)]
        for d in range(7):
            total = total + z_in[i][d]
        g, first = place(i)
        spot = s_sum.at[
            g, pl.ds(pl.multiple_of(first + r, 8), 8), pl.ds(pl.multiple_of(core * 512 + c, 128), width)
        ]
        spot[...] = total
        for d in range(1, 8):
            z_shares[i].append(send(spot, spot, zg_s.at[i, d - 1], zg_r.at[i, d - 1], z_peer[d - 1]))

    def share_x(i, whole=False):
        g, first = place(i)
        spot = s_sum.at[g, pl.ds(first, span(i)), mine]
        if whole:
            arrived(z_sends[i])
            total = z_full[0]
            for d in range(1, 8):
                total = total + z_full[d]
            spot[...] = total
        else:
            arrived(z_shares[i])
        for d in range(1, 4):
            x_shares[i].append(send(spot, spot, xg_s.at[i, d - 1], xg_r.at[i, d - 1], x_peer[d - 1]))

    def share_core(i):
        arrived(x_shares[i])
        for k, g in enumerate(SET_GROUPS[i]):
            spot = s_sum.at[g, :, mine]
            core_shares[i].append(send(spot, spot, cg_s.at[i, k], cg_r.at[i, k], other))

    def slot(a):
        return (a + Y_SIZE - y) % Y_SIZE

    g_rows = pl.ds(pl.multiple_of(core * 64, 64), 64)
    g_spot = pl.ds(pl.multiple_of(core * 64 + x * 16, 16), 16)

    def g_partial():
        ordered = [split(jnp.concatenate([v_all[2 * slot(a) + b] for a in range(4)], axis=0)) for b in range(2)]
        g_loc[...] = product(ordered[1], ordered[0], ((1,), (1,)))
        spot = g_loc.at[pl.ds(pl.multiple_of((1 - core) * 64, 64), 64)]
        core_copies[SETS].append(send(spot, g_core, c_s.at[4], c_r.at[4], other))

    def g_to_x():
        arrived(core_copies[SETS])
        g_loc[g_rows, :] = g_loc[g_rows, :] + g_core[...]
        for d in range(1, 4):
            spot = g_loc.at[pl.ds(pl.multiple_of(core * 64 + (x + d) % 4 * 16, 16), 16)]
            x_sends[SETS].append(
                send(spot, g_xin.at[d - 1], xs_s.at[SETS, d - 1], xs_r.at[SETS, d - 1], x_peer[d - 1])
            )

    def g_to_z():
        arrived(x_sends[SETS])
        g_zin[z] = (g_loc[g_spot, :] + g_xin[0]) + (g_xin[1] + g_xin[2])
        for d in range(1, 8):
            z_sends[SETS].append(
                send(g_zin.at[z], g_zin.at[z], zs_s.at[SETS, d - 1], zs_r.at[SETS, d - 1], z_peer[d - 1])
            )

    def g_share_x():
        arrived(z_sends[SETS])
        total = g_zin[0]
        for d in range(1, 8):
            total = total + g_zin[d]
        spot = g_sum.at[g_spot]
        spot[...] = total
        for d in range(1, 4):
            x_shares[SETS].append(send(spot, spot, xg_s.at[SETS, d - 1], xg_r.at[SETS, d - 1], x_peer[d - 1]))

    def g_share_core():
        arrived(x_shares[SETS])
        spot = g_sum.at[g_rows]
        core_shares[SETS].append(send(spot, spot, cg_s.at[SETS, 0], cg_r.at[SETS, 0], other))

    partial(0)
    from_down[0].wait_recv()
    opposite[0] = send(v_all.at[6], v_all.at[4], vs_sem.at[2, 0], vr_sem.at[2, 0], up)
    from_up[1].wait_recv()
    opposite[1] = send(v_all.at[3], v_all.at[5], vs_sem.at[2, 1], vr_sem.at[2, 1], down)
    partial(1)
    to_x(0)
    from_down[1].wait_recv()
    from_up[0].wait_recv()
    partial(2)
    to_z(0)
    to_x(1)
    opposite[0].wait_recv()
    opposite[1].wait_recv()
    partial(3)
    g_partial()
    to_z(1)
    to_x(2)
    g_to_x()
    share_z(0)
    to_z_whole(2)
    g_to_z()
    share_z(1)
    share_x(0)
    share_x(1)
    share_core(0)
    g_share_x()
    share_x(2, whole=True)
    share_core(1)
    g_share_core()
    share_core(2)

    factors.wait()
    upper = lax.broadcasted_iota(jnp.int32, (128, 128), 0) <= lax.broadcasted_iota(jnp.int32, (128, 128), 1)
    t0, t1 = (split(jnp.where(upper, f_ref[b], 0.0)) for b in range(2))
    for i in (0, 1, SETS, 2):
        arrived(core_shares[i])
    g = split(g_sum[...])

    for j in range(4):
        cols = pl.ds(j * 256, 256)
        s0, s1 = (jnp.concatenate([s_sum[2 * slot(a) + b, :, cols] for a in range(4)], axis=0) for b in range(2))
        c0 = split(product(t0, split(s0)))
        c1 = split(product(t1, split(s1 - product(g, c0))))
        for b, (high, low) in enumerate((c0, c1)):
            for a in range(4):
                ch_out[2 * slot(a) + b, :, cols] = high[a * 32 : (a + 1) * 32]
                cl_out[2 * slot(a) + b, :, cols] = low[a * 32 : (a + 1) * 32]

    for copy in kept:
        copy.wait()
    for copy in pending:
        copy.wait_send()


def update_kernel(x_ref, v_ref, ch_ref, cl_ref, out_ref):
    vh, vl = split(v_ref[...])
    dims = ((0,), (0,))
    ch = ch_ref[...]
    out_ref[...] = x_ref[...] - (dot(vh, ch, dims) + (dot(vh, cl_ref[...], dims) + dot(vl, ch, dims)))


def body(eigvecs, reflectors, factors):
    rows, columns = eigvecs.shape
    own = reflectors.transpose(0, 2, 1)
    group = own.shape[1]
    dma = pltpu.SemaphoreType.DMA
    any_space = pl.BlockSpec(memory_space=pl.ANY)
    vmem = pl.BlockSpec(memory_space=pltpu.VMEM)
    groups = Y_SIZE * BLOCKS
    heights = [group * len(groups_) for groups_ in SET_GROUPS]
    v_all, ch, cl = pl.pallas_call(
        reduce_kernel,
        out_shape=[
            jax.ShapeDtypeStruct((groups, group, rows), F32),
            jax.ShapeDtypeStruct((groups, group, columns), BF16),
            jax.ShapeDtypeStruct((groups, group, columns), BF16),
        ],
        in_specs=[any_space, any_space, any_space],
        out_specs=[any_space, vmem, vmem],
        scratch_shapes=[
            pltpu.VMEM((rows, columns), F32),
            pltpu.VMEM((rows, columns), BF16),
            pltpu.VMEM((rows, columns), BF16),
            pltpu.VMEM((groups, group, rows), F32),
            pltpu.VMEM(factors.shape, F32),
            [pltpu.VMEM((h, columns), F32) for h in heights],
            [pltpu.VMEM((h, 512), F32) for h in heights],
            [pltpu.VMEM((3, h // 4, 512), F32) for h in heights],
            [pltpu.VMEM((h // 4, 512), F32) for h in heights],
            [pltpu.VMEM((7, 8, 2 * h), F32) for h in heights],
            pltpu.VMEM((8, 16, 512), F32),
            pltpu.VMEM((groups, group, columns), F32),
            pltpu.VMEM((128, 128), F32),
            pltpu.VMEM((64, 128), F32),
            pltpu.VMEM((3, 16, 128), F32),
            pltpu.VMEM((8, 16, 128), F32),
            pltpu.VMEM((128, 128), F32),
            dma((CHUNKS,)), dma((2,)), dma((groups,)), dma((3, 2)), dma((3, 2)),
            dma((5,)), dma((5,)),
            dma((SETS + 1, 3)), dma((SETS + 1, 3)),
            dma((SETS + 1, 7)), dma((SETS + 1, 7)),
            dma((SETS, 7)), dma((SETS, 7)),
            dma((SETS + 1, 3)), dma((SETS + 1, 3)),
            dma((SETS + 1, 4)), dma((SETS + 1, 4)),
        ],
        compiler_params=pltpu.CompilerParams(
            collective_id=0, has_side_effects=True, vmem_limit_bytes=40 * 2**20
        ),
        name="gather_and_reduce",
    )(*(pltpu.with_memory_space_constraint(operand, pltpu.HBM) for operand in (eigvecs, own, factors)))

    depth = groups * group
    step = 256
    return pl.pallas_call(
        update_kernel,
        grid=(rows // step,),
        out_shape=jax.ShapeDtypeStruct((rows, columns), F32),
        in_specs=[
            pl.BlockSpec((step, columns), lambda i: (i, 0)),
            pl.BlockSpec((depth, step), lambda i: (0, i)),
            pl.BlockSpec((depth, columns), lambda i: (0, 0)),
            pl.BlockSpec((depth, columns), lambda i: (0, 0)),
        ],
        out_specs=pl.BlockSpec((step, columns), lambda i: (i, 0)),
        compiler_params=pltpu.CompilerParams(vmem_limit_bytes=32 * 2**20),
        name="update",
    )(eigvecs, v_all.reshape(depth, rows), ch.reshape(depth, columns), cl.reshape(depth, columns))


def solution(mesh):
    placed = (P("row", "col"), P(None, "row", "col"), P())
    return jax.shard_map(
        body, mesh=mesh, in_specs=placed, out_specs=P("row", "col"), check_vma=False
    )
```

time: 451 us -> 59.9 us (0.13)
  waiting for transfers between devices: 387 us -> 0 us
  Pallas kernels: 0 us -> 59.8 us
  matrix products: 33.5 us -> 0 us
  local copies, waits for them, and re-layouts: 16 us -> 0.01 us
  between operations: 13.2 us -> 0.02 us
    psum x2 -> x0, waiting for transfers between devices: 351 us -> none  [coefficients(): summed = lax.psum(partial_value, 'row')]
    pallas_call x0 -> x2, Pallas kernels: none -> 59.8 us  [the longest x1 54.4 us: body(): pl.pallas_call(reduce_kernel, out_shape=[jax.ShapeDtypeStruct((groups, gr...]
    all_gather x1 -> x0, waiting for transfers between devices: 34.8 us -> none  [body(): gathered = lax.all_gather(reflectors, 'col', axis=2, tiled=True)]
    dot_general x6 -> x0, matrix products: 33.5 us -> none  [product(): jnp.dot(left, right, precision=lax.Precision.HIGHEST, preferred_element_t...]
    unnamed x7 -> x2, local copies, waits for them, and re-layouts: 9.4 us -> 0.01 us
    sub x1 -> x0, local copies, waits for them, and re-layouts: 6.56 us -> none  [body(): vectors = vectors - product(householder, coefficient)]
  transfers between devices with their start and end apart: 3 -> 0, of which waited for: 3 -> 0; matrix products, arithmetic and copies ran while one was open for 2% -> 0% of each run, Pallas kernels for 0% -> 0%
where the time goes in v2:
time: 59.9 us; the launch traced here: 59.8 us
  Pallas kernels  59.8 us (100%)
    pallas_call x1, Pallas kernels, body(): pl.pallas_call(reduce_kernel, out_shape=[jax.ShapeDtypeStruct((groups, gr...  54.4 us
    pallas_call x1, Pallas kernels, body(): pl.pallas_call(update_kernel, grid=(rows // step,), out_shape=jax.ShapeDt...  5.43 us

profile of v2, /device:TPU:1, one launch (start us, length us, event | category | flops | bytes accessed | tf_op | source)
XLA Modules:
  0.0 59.8 jit_solution(12045042170085883334)
XLA Ops:
  0.0 0.0 copy-start
  0.0 54.4 %gather_and_reduce.1 = (f32[8,32,1536]{2,1,0:T(8,128)S(1)}, bf16[8,32,1024]{2,1,0:T(8,128)(2,1)S(1)}, bf16[8,32,1024]{2,1,0:T(8,128)(2,1)S(1)}) custom-call(f32[1536,1024]{1,0:T(8,128)} %x_ref.1, f32[2,32,1536]{2,1,0:T(8,128)} %bitcast.7, f32[2,128,128]{2,1,0:T(8,128)} %f_hbm.1), custom_call_target="tpu_custom_call" | custom-call | tf_op jit(solution)/shard_map/gather_and_reduce/pallas_call | solution.py:331
  54.4 0.0 copy-done
  54.4 5.4 %update.1 = f32[1536,1024]{1,0:T(8,128)} custom-call(f32[1536,1024]{1,0:T(8,128)S(1)} %copy-done, f32[256,1536]{1,0:T(8,128)S(1)} %bitcast.4, bf16[256,1024]{1,0:T(8,128)(2,1)S(1)} %bitcast.5, bf16[256,1024]{1,0:T(8,128)(2,1)S(1)} %bitcast.6), custom_call_target="tpu_custom_call" | custom-call | tf_op jit(solution)/shard_map/update/pallas_call | solution.py:374
Async XLA Ops:
  0.0 54.4 %copy-start = (f32[1536,1024]{1,0:T(8,128)S(1)}, f32[1536,1024]{1,0:T(8,128)}, u32[]{:S(2)}) copy-start(f32[1536,1024]{1,0:T(8,128)} %x_ref.1) | copy-start | bytes 18874372

commit v3 on v2

v3 whole, which is shorter than its diff:
```python
import jax
import jax.numpy as jnp
from jax import lax
from jax.experimental import pallas as pl
from jax.experimental.pallas import tpu as pltpu
from jax.sharding import PartitionSpec as P

MESH = pl.DeviceIdType.MESH
F32, BF16 = jnp.float32, jnp.bfloat16
BLOCKS = 2
Y_SIZE = 4
CHUNKS = 6

SET_GROUPS = ((0, 1), (6, 3), (7, 2), (4, 5))
SETS = len(SET_GROUPS)
STEPS = sorted(
    ((dz, dx) for dz in range(8) for dx in range(4) if dz or dx),
    key=lambda step: -min(step[0], 8 - step[0]) - min(step[1], 4 - step[1]),
)


def line(g):
    return g % 2 * 128 + g // 2 * 32


def split(value):
    high = value.astype(BF16)
    return high, (value - high.astype(F32)).astype(BF16)


def dot(left, right, dims):
    return lax.dot_general(left, right, (dims, ((), ())), preferred_element_type=F32)


def product(left, right, dims=((1,), (0,))):
    (lh, ll), (rh, rl) = left, right
    return dot(lh, rh, dims) + (dot(lh, rl, dims) + dot(ll, rh, dims))


def reduce_kernel(
    x_hbm, v_hbm, f_hbm, vh_out, vl_out, ch_out, cl_out,
    x_buf, xh, xl, v_all, vh_all, vl_all, vh_t, vl_t, f_ref, tri, s_loc, core_in, x_in, x_sum, z_in, d_in, s_sum, ch, cl,
    g_loc, g_core, g_xin, g_zin, g_sum,
    x_sem, v_sem, out_sem, vs_sem, vr_sem,
    c_s, c_r, xs_s, xs_r, zs_s, zs_r, zg_s, zg_r, xg_s, xg_r, cg_s, cg_r, ds_s, ds_r, dg_s, dg_r, entered,
):
    row, y = lax.axis_index("row"), lax.axis_index("col")
    z, x, core = row // 8, (row // 2) % 4, row % 2
    rows = x_hbm.shape[0] // CHUNKS

    def at(z_, x_, core_, y_):
        return ((z_ * 4 + x_) * 2 + core_, y_)

    other = at(z, x, 1 - core, y)
    x_peer = [at(z, (x + d) % 4, core, y) for d in range(1, 4)]
    z_peer = [at((z + d) % 8, x, core, y) for d in range(1, 8)]
    plane = [at((z + dz) % 8, (x + dx) % 4, core, y) for dz, dx in STEPS]
    y_peer = [at(z, x, core, (y + d) % 4) for d in range(1, 4)]
    up, down = y_peer[0], y_peer[2]
    mine = pl.ds(pl.multiple_of(core * 512, 512), 512)
    theirs = pl.ds(pl.multiple_of((1 - core) * 512, 512), 512)

    barrier = pltpu.get_barrier_semaphore()
    for device in y_peer + [other] + x_peer + z_peer:
        pl.semaphore_signal(barrier, inc=1, device_id=device, device_id_type=MESH)

    x_copies = []
    for i in range(CHUNKS):
        part = pl.ds(i * rows, rows)
        copy = pltpu.make_async_copy(x_hbm.at[part], x_buf.at[part], x_sem.at[i])
        copy.start()
        x_copies.append(copy)
    own = pltpu.make_async_copy(v_hbm, v_all.at[0:2], v_sem.at[0])
    own.start()
    factors = pltpu.make_async_copy(f_hbm, f_ref, v_sem.at[1])
    factors.start()

    def take(i):
        x_copies[i].wait()

        @pl.loop(0, rows // 64)
        def _(j):
            part = pl.ds(pl.multiple_of(i * rows + j * 64, 64), 64)
            high, low = split(x_buf[part, :])
            xh[part, :] = high
            xl[part, :] = low

    for i in range(CHUNKS // 2):
        take(i)

    pl.semaphore_wait(barrier, 14)

    pending = []

    def send(src, dst, s_sem, r_sem, device):
        copy = pltpu.make_async_remote_copy(
            src_ref=src, dst_ref=dst, send_sem=s_sem, recv_sem=r_sem, device_id=device, device_id_type=MESH
        )
        copy.start()
        pending.append(copy)
        return copy

    from_down, from_up, opposite = [None, None], [None, None], [None, None]
    for i in range(2):
        from_down[i] = send(v_hbm.at[i], v_all.at[6 + i], vs_sem.at[0, i], vr_sem.at[0, i], up)
        b = 1 - i
        from_up[b] = send(v_hbm.at[b], v_all.at[2 + b], vs_sem.at[1, b], vr_sem.at[1, b], down)

    for device in z_peer:
        pl.semaphore_signal(entered, inc=1, device_id=device, device_id_type=MESH)

    for i in range(CHUNKS // 2, CHUNKS):
        take(i)

    own.wait()

    core_copies, x_sends, z_sends, z_shares, x_shares, core_shares = ([[] for _ in range(SETS + 1)] for _ in range(6))

    def arrived(copies):
        while copies:
            copies.pop(0).wait_recv()

    def flush():
        while pending:
            pending.pop(0).wait_send()

    def partial(i):
        groups = SET_GROUPS[i]
        vh, vl = split(jnp.concatenate([v_all[g] for g in groups], axis=0))
        both = jnp.concatenate([vh, vl], axis=0)

        def columns(part):
            first = dot(both, xh[:, part], ((1,), (0,)))
            second = dot(vh, xl[:, part], ((1,), (0,)))
            s_loc[i, :, part] = first[:64] + (first[64:] + second)

        columns(theirs)
        core_copies[i].append(send(s_loc.at[i, :, theirs], core_in.at[i], c_s.at[i], c_r.at[i], other))
        columns(mine)
        for n, g in enumerate(groups):
            spot = slice(line(g), line(g) + 32)
            vh_all[spot] = vh[32 * n : 32 * n + 32]
            vl_all[spot] = vl[32 * n : 32 * n + 32]

    def add_core(i):
        arrived(core_copies[i])
        s_loc[i, :, mine] = s_loc[i, :, mine] + core_in[i]

    def group(i, half):
        first, second = SET_GROUPS[i]
        return first + half * (second - first)

    def x_rows(x_):
        return pl.ds(pl.multiple_of(x_ * 16, 16), 16)

    def z_tile(z_):
        return pl.ds(pl.multiple_of(z_ // 4 * 8, 8), 8), pl.multiple_of(z_ % 4 * 128, 128)

    def to_x(i):
        add_core(i)
        for d in range(1, 4):
            x_sends[i].append(
                send(
                    s_loc.at[i, x_rows((x + d) % 4), mine], x_in.at[i, d - 1],
                    xs_s.at[i, d - 1], xs_r.at[i, d - 1], x_peer[d - 1],
                )
            )

    def to_z(i):
        arrived(x_sends[i])
        x_sum[i] = (s_loc[i, x_rows(x), mine] + x_in[i, 0]) + (x_in[i, 1] + x_in[i, 2])
        for d in range(1, 8):
            r, c = z_tile((z + d) % 8)
            z_sends[i].append(
                send(
                    x_sum.at[i, r, pl.ds(c, 128)], z_in.at[i, d - 1],
                    zs_s.at[i, d - 1], zs_r.at[i, d - 1], z_peer[d - 1],
                )
            )

    def share_z(i):
        arrived(z_sends[i])
        r, c = z_tile(z)
        total = x_sum[i, r, pl.ds(c, 128)]
        for d in range(7):
            total = total + z_in[i, d]
        first = pl.multiple_of(x % 2 * 16 + z // 4 * 8, 8)
        spot = s_sum.at[group(i, x // 2), pl.ds(first, 8), pl.ds(pl.multiple_of(core * 512 + c, 128), 128)]
        spot[...] = total
        for d in range(1, 8):
            z_shares[i].append(send(spot, spot, zg_s.at[i, d - 1], zg_r.at[i, d - 1], z_peer[d - 1]))

    def share_x(i):
        arrived(z_shares[i])
        spot = s_sum.at[group(i, x // 2), pl.ds(pl.multiple_of(x % 2 * 16, 16), 16), mine]
        for d in range(1, 4):
            x_shares[i].append(send(spot, spot, xg_s.at[i, d - 1], xg_r.at[i, d - 1], x_peer[d - 1]))

    def tile(z_, x_):
        return pl.ds(pl.multiple_of(z_ * 8, 8), 8), pl.ds(pl.multiple_of(core * 512 + x_ * 128, 128), 128)

    def to_plane(i):
        add_core(i)
        for k, (dz, dx) in enumerate(STEPS):
            r, c = tile((z + dz) % 8, (x + dx) % 4)
            x_sends[i].append(
                send(s_loc.at[i, r, c], d_in.at[k], ds_s.at[k], ds_r.at[k], plane[k])
            )

    def share_plane(i):
        arrived(x_sends[i])
        r, c = tile(z, x)
        total = s_loc[i, r, c]
        for k in range(len(STEPS)):
            total = total + d_in[k]
        spot = s_sum.at[group(i, z // 4), pl.ds(pl.multiple_of(z % 4 * 8, 8), 8), c]
        spot[...] = total
        for k in range(len(STEPS)):
            x_shares[i].append(send(spot, spot, dg_s.at[k], dg_r.at[k], plane[k]))

    def share_core(i):
        arrived(x_shares[i])
        for k, g in enumerate(SET_GROUPS[i]):
            spot = s_sum.at[g, :, mine]
            core_shares[i].append(send(spot, spot, cg_s.at[i, k], cg_r.at[i, k], other))

    PAIRS = ((0, 0), (0, 3), (1, 3), (3, 0))
    g_half = pl.ds(pl.multiple_of(core * 16, 16), 16)
    g_other = pl.ds(pl.multiple_of((1 - core) * 16, 16), 16)

    def g_partial():
        second, first = (
            tuple(jnp.concatenate([v[line(g) : line(g) + 32] for g in groups], axis=0) for v in (vh_all, vl_all))
            for groups in ((1, 3, 7), (0, 6))
        )
        pairs = product(second, first, ((1,), (1,)))
        place = {0: 0, 1: 1, 3: 2}, {0: 0, 3: 1}
        g_loc[...] = jnp.concatenate(
            [
                pairs[32 * place[0][i] : 32 * place[0][i] + 32, 32 * place[1][j] : 32 * place[1][j] + 32]
                for i, j in PAIRS
            ],
            axis=1,
        )
        core_copies[SETS].append(send(g_loc.at[g_other], g_core, c_s.at[SETS], c_r.at[SETS], other))

    def g_to_x():
        arrived(core_copies[SETS])
        g_xin[x] = g_loc[g_half, :] + g_core[...]
        for d in range(1, 4):
            x_sends[SETS].append(
                send(g_xin.at[x], g_xin.at[x], xs_s.at[SETS, d - 1], xs_r.at[SETS, d - 1], x_peer[d - 1])
            )

    def g_to_z():
        arrived(x_sends[SETS])
        g_zin[z] = (g_xin[0] + g_xin[1]) + (g_xin[2] + g_xin[3])
        for d in range(1, 8):
            z_sends[SETS].append(
                send(g_zin.at[z], g_zin.at[z], zs_s.at[SETS, d - 1], zs_r.at[SETS, d - 1], z_peer[d - 1])
            )

    def g_share_core():
        arrived(z_sends[SETS])
        total = g_zin[0]
        for d in range(1, 8):
            total = total + g_zin[d]
        spot = g_sum.at[0, g_half]
        spot[...] = total
        core_shares[SETS].append(send(spot, spot, cg_s.at[SETS, 0], cg_r.at[SETS, 0], other))

    def g_share_y():
        arrived(core_shares[SETS])
        for d in range(1, 4):
            x_shares[SETS].append(
                send(g_sum.at[0], g_sum.at[4 - d], xg_s.at[SETS, d - 1], xg_r.at[SETS, d - 1], y_peer[d - 1])
            )

    def g_whole():
        arrived(x_shares[SETS])
        lines = []
        for i in range(4):
            blocks = []
            for j in range(4):
                d = (i - j) % 4
                source = (i, i, i + 3, i + 1)[d] % 4
                blocks.append(g_sum[source, :, 32 * d : 32 * d + 32])
            lines.append(jnp.concatenate(blocks, axis=1))
        return jnp.concatenate(lines, axis=0)

    outs = []

    def leave(src, dst):
        copy = pltpu.make_async_copy(src, dst, out_sem.at[len(outs)])
        copy.start()
        outs.append(copy)

    partial(0)
    to_x(0)

    factors.wait()
    upper = lax.broadcasted_iota(jnp.int32, (128, 128), 0) <= lax.broadcasted_iota(jnp.int32, (128, 128), 1)
    turn = (Y_SIZE - y) % Y_SIZE * 32
    for b in range(2):
        tri[b] = pltpu.roll(pltpu.roll(jnp.where(upper, f_ref[b], 0.0), turn, 0), turn, 1)

    from_down[0].wait_recv()
    opposite[0] = send(v_all.at[6], v_all.at[4], vs_sem.at[2, 0], vr_sem.at[2, 0], up)
    from_up[1].wait_recv()
    opposite[1] = send(v_all.at[3], v_all.at[5], vs_sem.at[2, 1], vr_sem.at[2, 1], down)
    partial(1)
    to_z(0)
    to_x(1)
    from_down[1].wait_recv()
    from_up[0].wait_recv()
    partial(2)
    g_partial()
    to_x(2)
    share_z(0)
    to_z(1)
    g_to_x()
    pl.semaphore_wait(entered, 7)
    opposite[0].wait_recv()
    opposite[1].wait_recv()
    partial(3)
    to_plane(3)
    to_z(2)
    g_to_z()
    share_x(0)
    share_z(1)

    @pl.loop(0, CHUNKS)
    def _(i):
        part = pl.ds(pl.multiple_of(i * rows, rows), rows)
        vh_t[part, :] = vh_all[:, part].T
        vl_t[part, :] = vl_all[:, part].T

    leave(vh_t, vh_out)
    leave(vl_t, vl_out)

    share_core(0)
    share_z(2)
    g_share_core()
    share_x(1)
    g_share_y()
    share_plane(3)
    share_x(2)
    share_core(1)
    share_core(2)
    for i in range(3):
        arrived(core_shares[i])

    t0, t1 = split(tri[0]), split(tri[1])
    mixed = product(split(product(t1, split(g_whole()))), t0)
    matrix = split(
        jnp.concatenate(
            [
                jnp.concatenate([tri[0], jnp.zeros((128, 128), F32)], axis=1),
                jnp.concatenate([-mixed, tri[1]], axis=1),
            ],
            axis=0,
        )
    )
    flush()
    share_core(3)
    arrived(core_shares[3])
    for j in range(4):
        cols = pl.ds(j * 256, 256)
        sums = jnp.concatenate([s_sum[n, :, cols] for n in (0, 2, 4, 6, 1, 3, 5, 7)], axis=0)
        ch[:, cols], cl[:, cols] = split(product(matrix, split(sums)))
        leave(ch.at[:, cols], ch_out.at[:, cols])
        leave(cl.at[:, cols], cl_out.at[:, cols])

    for copy in outs:
        copy.wait()
    flush()


def update_kernel(x_ref, vh_ref, vl_ref, ch_ref, cl_ref, out, buffer, sem):
    step = x_ref.shape[0] // CHUNKS
    copies = []
    for i in range(CHUNKS):
        part = pl.ds(i * step, step)
        for j in range(4):
            cols = pl.ds(j * 256, 256)
            change = product((vh_ref[part, :], vl_ref[part, :]), (ch_ref[:, cols], cl_ref[:, cols]))
            buffer[part, cols] = x_ref[part, cols] - change
        copy = pltpu.make_async_copy(buffer.at[part], out.at[part], sem.at[i])
        copy.start()
        copies.append(copy)
    for copy in copies:
        copy.wait()


def body(eigvecs, reflectors, factors):
    rows, columns = eigvecs.shape
    own = reflectors.transpose(0, 2, 1)
    group = own.shape[1]
    dma = pltpu.SemaphoreType.DMA
    any_space = pl.BlockSpec(memory_space=pl.ANY)
    groups = Y_SIZE * BLOCKS
    depth = groups * group
    vh, vl, ch, cl = pl.pallas_call(
        reduce_kernel,
        out_shape=[
            jax.ShapeDtypeStruct((rows, depth), BF16),
            jax.ShapeDtypeStruct((rows, depth), BF16),
            jax.ShapeDtypeStruct((depth, columns), BF16),
            jax.ShapeDtypeStruct((depth, columns), BF16),
        ],
        in_specs=[any_space, any_space, any_space],
        out_specs=[any_space, any_space, any_space, any_space],
        scratch_shapes=[
            pltpu.VMEM((rows, columns), F32),
            pltpu.VMEM((rows, columns), BF16),
            pltpu.VMEM((rows, columns), BF16),
            pltpu.VMEM((groups, group, rows), F32),
            pltpu.VMEM((depth, rows), BF16),
            pltpu.VMEM((depth, rows), BF16),
            pltpu.VMEM((rows, depth), BF16),
            pltpu.VMEM((rows, depth), BF16),
            pltpu.VMEM(factors.shape, F32),
            pltpu.VMEM(factors.shape, F32),
            pltpu.VMEM((SETS, 64, columns), F32),
            pltpu.VMEM((SETS, 64, 512), F32),
            pltpu.VMEM((SETS - 1, 3, 16, 512), F32),
            pltpu.VMEM((SETS - 1, 16, 512), F32),
            pltpu.VMEM((SETS - 1, 7, 8, 128), F32),
            pltpu.VMEM((len(STEPS), 8, 128), F32),
            pltpu.VMEM((groups, group, columns), F32),
            pltpu.VMEM((depth, columns), BF16),
            pltpu.VMEM((depth, columns), BF16),
            pltpu.VMEM((32, 128), F32),
            pltpu.VMEM((16, 128), F32),
            pltpu.VMEM((4, 16, 128), F32),
            pltpu.VMEM((8, 16, 128), F32),
            pltpu.VMEM((4, 32, 128), F32),
            dma((CHUNKS,)), dma((2,)), dma((10,)), dma((3, 2)), dma((3, 2)),
            dma((SETS + 1,)), dma((SETS + 1,)),
            dma((SETS + 1, 3)), dma((SETS + 1, 3)),
            dma((SETS + 1, 7)), dma((SETS + 1, 7)),
            dma((SETS, 7)), dma((SETS, 7)),
            dma((SETS + 1, 3)), dma((SETS + 1, 3)),
            dma((SETS + 1, 2)), dma((SETS + 1, 2)),
            dma((len(STEPS),)), dma((len(STEPS),)),
            dma((len(STEPS),)), dma((len(STEPS),)),
            pltpu.SemaphoreType.REGULAR,
        ],
        compiler_params=pltpu.CompilerParams(
            collective_id=0, has_side_effects=True, vmem_limit_bytes=40 * 2**20
        ),
        name="gather_and_reduce",
    )(*(pltpu.with_memory_space_constraint(operand, pltpu.HBM) for operand in (eigvecs, own, factors)))

    operands = (eigvecs, vh, vl, ch, cl)
    return pl.pallas_call(
        update_kernel,
        out_shape=jax.ShapeDtypeStruct((rows, columns), F32),
        in_specs=[pl.BlockSpec(memory_space=pltpu.VMEM)] * len(operands),
        out_specs=any_space,
        scratch_shapes=[pltpu.VMEM((rows, columns), F32), dma((CHUNKS,))],
        compiler_params=pltpu.CompilerParams(vmem_limit_bytes=16 * 2**20),
        name="update",
    )(*(pltpu.with_memory_space_constraint(operand, pltpu.VMEM) for operand in operands))


def solution(mesh):
    placed = (P("row", "col"), P(None, "row", "col"), P())
    return jax.shard_map(
        body, mesh=mesh, in_specs=placed, out_specs=P("row", "col"), check_vma=False
    )
```

time: 59.9 us -> 55.4 us (0.925)
  Pallas kernels: 59.8 us -> 55.3 us
    pallas_call x2, Pallas kernels: 59.8 us -> 55.3 us  [the longest x1 51.6 us: body(): pl.pallas_call(reduce_kernel, out_shape=[jax.ShapeDtypeStruct((rows, dept...]
where the time goes in v3:
time: 55.4 us; the launch traced here: 55.3 us
  Pallas kernels  55.3 us (100%)
    pallas_call x1, Pallas kernels, body(): pl.pallas_call(reduce_kernel, out_shape=[jax.ShapeDtypeStruct((rows, dept...  51.6 us
    pallas_call x1, Pallas kernels, body(): pl.pallas_call(update_kernel, out_shape=jax.ShapeDtypeStruct((rows, colum...  3.64 us

profile of v3, /device:TPU:1, one launch (start us, length us, event | category | flops | bytes accessed | tf_op | source)
XLA Modules:
  0.0 55.3 jit_solution(13428454497470331336)
XLA Ops:
  0.0 0.0 copy-start
  0.0 51.6 %gather_and_reduce.1 = (bf16[1536,256]{1,0:T(8,128)(2,1)S(1)}, bf16[1536,256]{1,0:T(8,128)(2,1)S(1)}, bf16[256,1024]{1,0:T(8,128)(2,1)S(1)}, bf16[256,1024]{1,0:T(8,128)(2,1)S(1)}) custom-call(f32[1536,1024]{1,0:T(8,128)} %x_ref.1, f32[2,32,1536]{2,1,0:T(8,128)} %bitcast.1, f32[2,128,128]{2,1,0:T(8,128)} %f_hbm.1), custom_call_target="tpu_custom_call" | custom-call | tf_op jit(solution)/shard_map/gather_and_reduce/pallas_call | solution.py:403
  51.7 0.0 copy-done
  51.7 3.6 %update.1 = f32[1536,1024]{1,0:T(8,128)} custom-call(f32[1536,1024]{1,0:T(8,128)S(1)} %copy-done, bf16[1536,256]{1,0:T(8,128)(2,1)S(1)} %get-tuple-element.9.vh_ref, bf16[1536,256]{1,0:T(8,128)(2,1)S(1)} %get-tuple-element.10.vl_ref, bf16[256,1024]{1,0:T(8,128)(2,1)S(1)} %get-tuple-element.11.ch_ref, bf16[256,1024]{1,0:T(8,128)(2,1)S(1)} %get-tuple-element.12.cl_ref), custom_call_target="tpu_custom_call" | custom-call | tf_op jit(solution)/shard_map/update/pallas_call | solution.py:456
Async XLA Ops:
  0.0 51.7 %copy-start = (f32[1536,1024]{1,0:T(8,128)S(1)}, f32[1536,1024]{1,0:T(8,128)}, u32[]{:S(2)}) copy-start(f32[1536,1024]{1,0:T(8,128)} %x_ref.1) | copy-start | bytes 18874372

commit v4 on v3

--- a/solution.py
+++ b/solution.py
@@ -10,6 +10,7 @@
 BLOCKS = 2
 Y_SIZE = 4
 CHUNKS = 6
+PIECES = 12
 
 SET_GROUPS = ((0, 1), (6, 3), (7, 2), (4, 5))
 SETS = len(SET_GROUPS)
@@ -39,10 +40,10 @@
 
 def reduce_kernel(
     x_hbm, v_hbm, f_hbm, vh_out, vl_out, ch_out, cl_out,
-    x_buf, xh, xl, v_all, vh_all, vl_all, vh_t, vl_t, f_ref, tri, s_loc, core_in, x_in, x_sum, z_in, d_in, s_sum, ch, cl,
+    x_buf, xh, xl, v_all, vh_all, vl_all, vh_t, vl_t, f_ref, tri, s_loc, core_in, x_in, x_sum, z_in, d_in, s_sum, c_part, ch, cl,
     g_loc, g_core, g_xin, g_zin, g_sum,
     x_sem, v_sem, out_sem, vs_sem, vr_sem,
-    c_s, c_r, xs_s, xs_r, zs_s, zs_r, zg_s, zg_r, xg_s, xg_r, cg_s, cg_r, ds_s, ds_r, dg_s, dg_r, entered,
+    c_s, c_r, xs_s, xs_r, zs_s, zs_r, zg_s, zg_r, xg_s, xg_r, cg_s, cg_r, ds_s, ds_r, dg_s, dg_r, greeted,
 ):
     row, y = lax.axis_index("row"), lax.axis_index("col")
     z, x, core = row // 8, (row // 2) % 4, row % 2
@@ -60,16 +61,17 @@
     mine = pl.ds(pl.multiple_of(core * 512, 512), 512)
     theirs = pl.ds(pl.multiple_of((1 - core) * 512, 512), 512)
 
+    z_near = [at((z + d) % 8, x, core, y) for d in (1, 7)]
+    z_next = [at((z + d) % 8, x, core, y) for d in (2, 6)]
+    x_near = [x_peer[0], x_peer[2]]
+
+    def greet(semaphore, devices):
+        for device in devices:
+            pl.semaphore_signal(semaphore, inc=1, device_id=device, device_id_type=MESH)
+
     barrier = pltpu.get_barrier_semaphore()
-    for device in y_peer + [other] + x_peer + z_peer:
-        pl.semaphore_signal(barrier, inc=1, device_id=device, device_id_type=MESH)
-
-    x_copies = []
-    for i in range(CHUNKS):
-        part = pl.ds(i * rows, rows)
-        copy = pltpu.make_async_copy(x_hbm.at[part], x_buf.at[part], x_sem.at[i])
-        copy.start()
-        x_copies.append(copy)
+    greet(barrier, [up, down, other] + x_near + z_near)
+
     own = pltpu.make_async_copy(v_hbm, v_all.at[0:2], v_sem.at[0])
     own.start()
     factors = pltpu.make_async_copy(f_hbm, f_ref, v_sem.at[1])
@@ -85,11 +87,8 @@
             xh[part, :] = high
             xl[part, :] = low
 
-    for i in range(CHUNKS // 2):
-        take(i)
-
-    pl.semaphore_wait(barrier, 14)
-
+    own.wait()
+    pl.semaphore_wait(barrier, 7)
     pending = []
 
     def send(src, dst, s_sem, r_sem, device):
@@ -102,17 +101,23 @@
 
     from_down, from_up, opposite = [None, None], [None, None], [None, None]
     for i in range(2):
-        from_down[i] = send(v_hbm.at[i], v_all.at[6 + i], vs_sem.at[0, i], vr_sem.at[0, i], up)
+        from_down[i] = send(v_all.at[i], v_all.at[6 + i], vs_sem.at[0, i], vr_sem.at[0, i], up)
         b = 1 - i
-        from_up[b] = send(v_hbm.at[b], v_all.at[2 + b], vs_sem.at[1, b], vr_sem.at[1, b], down)
-
-    for device in z_peer:
-        pl.semaphore_signal(entered, inc=1, device_id=device, device_id_type=MESH)
-
-    for i in range(CHUNKS // 2, CHUNKS):
+        from_up[b] = send(v_all.at[b], v_all.at[2 + b], vs_sem.at[1, b], vr_sem.at[1, b], down)
+
+    x_copies = []
+    for i in range(CHUNKS):
+        part = pl.ds(i * rows, rows)
+        copy = pltpu.make_async_copy(x_hbm.at[part], x_buf.at[part], x_sem.at[i])
+        copy.start()
+        x_copies.append(copy)
+    greet(greeted.at[0], z_near)
+    greet(greeted.at[1], x_near)
+    for i in range(CHUNKS):
         take(i)
-
-    own.wait()
+        if i == 2:
+            pl.semaphore_wait(greeted.at[0], 2)
+            greet(greeted.at[2], z_next)
 
     core_copies, x_sends, z_sends, z_shares, x_shares, core_shares = ([[] for _ in range(SETS + 1)] for _ in range(6))
 
@@ -120,8 +125,8 @@
         while copies:
             copies.pop(0).wait_recv()
 
-    def flush():
-        while pending:
+    def flush(left=0):
+        while len(pending) > left:
             pending.pop(0).wait_send()
 
     def partial(i):
@@ -204,7 +209,7 @@
         for k, (dz, dx) in enumerate(STEPS):
             r, c = tile((z + dz) % 8, (x + dx) % 4)
             x_sends[i].append(
-                send(s_loc.at[i, r, c], d_in.at[k], ds_s.at[k], ds_r.at[k], plane[k])
+                send(s_loc.at[i, r, c], d_in.at[i - 2, k], ds_s.at[i - 2, k], ds_r.at[i - 2, k], plane[k])
             )
 
     def share_plane(i):
@@ -212,11 +217,11 @@
         r, c = tile(z, x)
         total = s_loc[i, r, c]
         for k in range(len(STEPS)):
-            total = total + d_in[k]
+            total = total + d_in[i - 2, k]
         spot = s_sum.at[group(i, z // 4), pl.ds(pl.multiple_of(z % 4 * 8, 8), 8), c]
         spot[...] = total
         for k in range(len(STEPS)):
-            x_shares[i].append(send(spot, spot, dg_s.at[k], dg_r.at[k], plane[k]))
+            x_shares[i].append(send(spot, spot, dg_s.at[i - 2, k], dg_r.at[i - 2, k], plane[k]))
 
     def share_core(i):
         arrived(x_shares[i])
@@ -296,7 +301,17 @@
         outs.append(copy)
 
     partial(0)
+    pl.semaphore_wait(greeted.at[1], 2)
     to_x(0)
+    pl.semaphore_wait(greeted.at[2], 2)
+    greet(greeted.at[3], z_peer)
+
+    from_down[0].wait_recv()
+    opposite[0] = send(v_all.at[6], v_all.at[4], vs_sem.at[2, 0], vr_sem.at[2, 0], up)
+    from_up[1].wait_recv()
+    opposite[1] = send(v_all.at[3], v_all.at[5], vs_sem.at[2, 1], vr_sem.at[2, 1], down)
+    partial(1)
+    to_x(1)
 
     factors.wait()
     upper = lax.broadcasted_iota(jnp.int32, (128, 128), 0) <= lax.broadcasted_iota(jnp.int32, (128, 128), 1)
@@ -304,30 +319,24 @@
     for b in range(2):
         tri[b] = pltpu.roll(pltpu.roll(jnp.where(upper, f_ref[b], 0.0), turn, 0), turn, 1)
 
-    from_down[0].wait_recv()
-    opposite[0] = send(v_all.at[6], v_all.at[4], vs_sem.at[2, 0], vr_sem.at[2, 0], up)
-    from_up[1].wait_recv()
-    opposite[1] = send(v_all.at[3], v_all.at[5], vs_sem.at[2, 1], vr_sem.at[2, 1], down)
-    partial(1)
-    to_z(0)
-    to_x(1)
     from_down[1].wait_recv()
     from_up[0].wait_recv()
     partial(2)
+    to_z(0)
     g_partial()
-    to_x(2)
-    share_z(0)
+    pl.semaphore_wait(greeted.at[3], 7)
+    to_plane(2)
+    g_to_x()
     to_z(1)
-    g_to_x()
-    pl.semaphore_wait(entered, 7)
     opposite[0].wait_recv()
     opposite[1].wait_recv()
     partial(3)
     to_plane(3)
-    to_z(2)
+    share_z(0)
     g_to_z()
+    share_z(1)
+    share_plane(2)
     share_x(0)
-    share_z(1)
 
     @pl.loop(0, CHUNKS)
     def _(i):
@@ -335,20 +344,16 @@
         vh_t[part, :] = vh_all[:, part].T
         vl_t[part, :] = vl_all[:, part].T
 
+    flush(40)
     leave(vh_t, vh_out)
     leave(vl_t, vl_out)
 
-    share_core(0)
-    share_z(2)
+    share_plane(3)
     g_share_core()
     share_x(1)
     g_share_y()
-    share_plane(3)
-    share_x(2)
-    share_core(1)
+    share_core(0)
     share_core(2)
-    for i in range(3):
-        arrived(core_shares[i])
 
     t0, t1 = split(tri[0]), split(tri[1])
     mixed = product(split(product(t1, split(g_whole()))), t0)
@@ -361,15 +366,39 @@
             axis=0,
         )
     )
-    flush()
+
+    def part_of(i):
+        high, low = matrix
+        return jnp.concatenate([m[:, line(g) : line(g) + 32] for m in (high, high, low) for g in SET_GROUPS[i]], axis=1)
+
+    def term(i, wide, cols):
+        sh, sl = split(jnp.concatenate([s_sum[g, :, cols] for g in SET_GROUPS[i]], axis=0))
+        return dot(wide, jnp.concatenate([sh, sl, sh], axis=0), ((1,), (0,)))
+
+    def add_set(i, first=False):
+        arrived(core_shares[i])
+        wide = part_of(i)
+        for j in range(4):
+            cols = pl.ds(j * 256, 256)
+            c_part[:, cols] = term(i, wide, cols) if first else c_part[:, cols] + term(i, wide, cols)
+
+    def finish(start, wide):
+        for j in range(2):
+            cols = pl.ds(pl.multiple_of(start + j * 256, 256), 256)
+            ch[:, cols], cl[:, cols] = split(c_part[:, cols] + term(3, wide, cols))
+            leave(ch.at[:, cols], ch_out.at[:, cols])
+            leave(cl.at[:, cols], cl_out.at[:, cols])
+
+    add_set(0, first=True)
+    share_core(1)
+    flush(40)
+    add_set(2)
     share_core(3)
+    add_set(1)
+    wide = part_of(3)
+    finish(core * 512, wide)
     arrived(core_shares[3])
-    for j in range(4):
-        cols = pl.ds(j * 256, 256)
-        sums = jnp.concatenate([s_sum[n, :, cols] for n in (0, 2, 4, 6, 1, 3, 5, 7)], axis=0)
-        ch[:, cols], cl[:, cols] = split(product(matrix, split(sums)))
-        leave(ch.at[:, cols], ch_out.at[:, cols])
-        leave(cl.at[:, cols], cl_out.at[:, cols])
+    finish((1 - core) * 512, wide)
 
     for copy in outs:
         copy.wait()
@@ -377,9 +406,9 @@
 
 
 def update_kernel(x_ref, vh_ref, vl_ref, ch_ref, cl_ref, out, buffer, sem):
-    step = x_ref.shape[0] // CHUNKS
+    step = x_ref.shape[0] // PIECES
     copies = []
-    for i in range(CHUNKS):
+    for i in range(PIECES):
         part = pl.ds(i * step, step)
         for j in range(4):
             cols = pl.ds(j * 256, 256)
@@ -426,8 +455,9 @@
             pltpu.VMEM((SETS - 1, 3, 16, 512), F32),
             pltpu.VMEM((SETS - 1, 16, 512), F32),
             pltpu.VMEM((SETS - 1, 7, 8, 128), F32),
-            pltpu.VMEM((len(STEPS), 8, 128), F32),
+            pltpu.VMEM((2, len(STEPS), 8, 128), F32),
             pltpu.VMEM((groups, group, columns), F32),
+            pltpu.VMEM((depth, columns), F32),
             pltpu.VMEM((depth, columns), BF16),
             pltpu.VMEM((depth, columns), BF16),
             pltpu.VMEM((32, 128), F32),
@@ -442,9 +472,9 @@
             dma((SETS, 7)), dma((SETS, 7)),
             dma((SETS + 1, 3)), dma((SETS + 1, 3)),
             dma((SETS + 1, 2)), dma((SETS + 1, 2)),
-            dma((len(STEPS),)), dma((len(STEPS),)),
-            dma((len(STEPS),)), dma((len(STEPS),)),
-            pltpu.SemaphoreType.REGULAR,
+            dma((2, len(STEPS))), dma((2, len(STEPS))),
+            dma((2, len(STEPS))), dma((2, len(STEPS))),
+            pltpu.SemaphoreType.REGULAR((4,)),
         ],
         compiler_params=pltpu.CompilerParams(
             collective_id=0, has_side_effects=True, vmem_limit_bytes=40 * 2**20
@@ -458,7 +488,7 @@
         out_shape=jax.ShapeDtypeStruct((rows, columns), F32),
         in_specs=[pl.BlockSpec(memory_space=pltpu.VMEM)] * len(operands),
         out_specs=any_space,
-        scratch_shapes=[pltpu.VMEM((rows, columns), F32), dma((CHUNKS,))],
+        scratch_shapes=[pltpu.VMEM((rows, columns), F32), dma((PIECES,))],
         compiler_params=pltpu.CompilerParams(vmem_limit_bytes=16 * 2**20),
         name="update",
     )(*(pltpu.with_memory_space_constraint(operand, pltpu.VMEM) for operand in operands))

time: 55.4 us -> 52.3 us (0.944)
  Pallas kernels: 55.3 us -> 52.2 us
    pallas_call x1, Pallas kernels: 51.6 us -> 48.6 us  [body(): pl.pallas_call(reduce_kernel, out_shape=[jax.ShapeDtypeStruct((rows, dept...]
where the time goes in v4:
time: 52.3 us; the launch traced here: 52.2 us
  Pallas kernels  52.2 us (100%)
    pallas_call x1, Pallas kernels, body(): pl.pallas_call(reduce_kernel, out_shape=[jax.ShapeDtypeStruct((rows, dept...  48.6 us
    pallas_call x1, Pallas kernels, body(): pl.pallas_call(update_kernel, out_shape=jax.ShapeDtypeStruct((rows, colum...  3.54 us

profile of v4, /device:TPU:1, one launch (start us, length us, event | category | flops | bytes accessed | tf_op | source)
XLA Modules:
  0.0 52.2 jit_solution(8705765476953583962)
XLA Ops:
  0.0 0.0 copy-start
  0.0 48.6 %gather_and_reduce.1 = (bf16[1536,256]{1,0:T(8,128)(2,1)S(1)}, bf16[1536,256]{1,0:T(8,128)(2,1)S(1)}, bf16[256,1024]{1,0:T(8,128)(2,1)S(1)}, bf16[256,1024]{1,0:T(8,128)(2,1)S(1)}) custom-call(f32[1536,1024]{1,0:T(8,128)} %x_ref.1, f32[2,32,1536]{2,1,0:T(8,128)} %bitcast.1, f32[2,128,128]{2,1,0:T(8,128)} %f_hbm.1), custom_call_target="tpu_custom_call" | custom-call | tf_op jit(solution)/shard_map/gather_and_reduce/pallas_call | solution.py:432
  48.7 0.0 copy-done
  48.7 3.5 %update.1 = f32[1536,1024]{1,0:T(8,128)} custom-call(f32[1536,1024]{1,0:T(8,128)S(1)} %copy-done, bf16[1536,256]{1,0:T(8,128)(2,1)S(1)} %get-tuple-element.9.vh_ref, bf16[1536,256]{1,0:T(8,128)(2,1)S(1)} %get-tuple-element.10.vl_ref, bf16[256,1024]{1,0:T(8,128)(2,1)S(1)} %get-tuple-element.11.ch_ref, bf16[256,1024]{1,0:T(8,128)(2,1)S(1)} %get-tuple-element.12.cl_ref), custom_call_target="tpu_custom_call" | custom-call | tf_op jit(solution)/shard_map/update/pallas_call | solution.py:486
Async XLA Ops:
  0.0 48.7 %copy-start = (f32[1536,1024]{1,0:T(8,128)S(1)}, f32[1536,1024]{1,0:T(8,128)}, u32[]{:S(2)}) copy-start(f32[1536,1024]{1,0:T(8,128)} %x_ref.1) | copy-start | bytes 18874372

commit v5 on v4

--- a/solution.py
+++ b/solution.py
@@ -307,10 +307,10 @@
     greet(greeted.at[3], z_peer)
 
     from_down[0].wait_recv()
+    from_up[1].wait_recv()
+    partial(1)
     opposite[0] = send(v_all.at[6], v_all.at[4], vs_sem.at[2, 0], vr_sem.at[2, 0], up)
-    from_up[1].wait_recv()
     opposite[1] = send(v_all.at[3], v_all.at[5], vs_sem.at[2, 1], vr_sem.at[2, 1], down)
-    partial(1)
     to_x(1)
 
     factors.wait()

time: 52.3 us -> 51.7 us (0.989)
    pallas_call x1, Pallas kernels: 48.6 us -> 48.1 us  [body(): pl.pallas_call(reduce_kernel, out_shape=[jax.ShapeDtypeStruct((rows, dept...]
where the time goes in v5:
time: 51.7 us
  Pallas kernels  51.7 us (100%)
    pallas_call x1, Pallas kernels, body(): pl.pallas_call(reduce_kernel, out_shape=[jax.ShapeDtypeStruct((rows, dept...  48.1 us
    pallas_call x1, Pallas kernels, body(): pl.pallas_call(update_kernel, out_shape=jax.ShapeDtypeStruct((rows, colum...  3.54 us

profile of v5, /device:TPU:1, one launch (start us, length us, event | category | flops | bytes accessed | tf_op | source)
XLA Modules:
  0.0 51.7 jit_solution(8325138551372175137)
XLA Ops:
  0.0 0.0 copy-start
  0.0 48.1 %gather_and_reduce.1 = (bf16[1536,256]{1,0:T(8,128)(2,1)S(1)}, bf16[1536,256]{1,0:T(8,128)(2,1)S(1)}, bf16[256,1024]{1,0:T(8,128)(2,1)S(1)}, bf16[256,1024]{1,0:T(8,128)(2,1)S(1)}) custom-call(f32[1536,1024]{1,0:T(8,128)} %x_ref.1, f32[2,32,1536]{2,1,0:T(8,128)} %bitcast.1, f32[2,128,128]{2,1,0:T(8,128)} %f_hbm.1), custom_call_target="tpu_custom_call" | custom-call | tf_op jit(solution)/shard_map/gather_and_reduce/pallas_call | solution.py:432
  48.1 0.0 copy-done
  48.1 3.5 %update.1 = f32[1536,1024]{1,0:T(8,128)} custom-call(f32[1536,1024]{1,0:T(8,128)S(1)} %copy-done, bf16[1536,256]{1,0:T(8,128)(2,1)S(1)} %get-tuple-element.9.vh_ref, bf16[1536,256]{1,0:T(8,128)(2,1)S(1)} %get-tuple-element.10.vl_ref, bf16[256,1024]{1,0:T(8,128)(2,1)S(1)} %get-tuple-element.11.ch_ref, bf16[256,1024]{1,0:T(8,128)(2,1)S(1)} %get-tuple-element.12.cl_ref), custom_call_target="tpu_custom_call" | custom-call | tf_op jit(solution)/shard_map/update/pallas_call | solution.py:486
Async XLA Ops:
  0.0 48.1 %copy-start = (f32[1536,1024]{1,0:T(8,128)S(1)}, f32[1536,1024]{1,0:T(8,128)}, u32[]{:S(2)}) copy-start(f32[1536,1024]{1,0:T(8,128)} %x_ref.1) | copy-start | bytes 18874372
